TPU v7x, 32 devices: a whole 2x2x4 slice. The times are simulated.
32 devices in a mesh: row: 4 (over x, core), col: 8 (over z, y).
Axes of the slice: x: 2, y: 2, z: 4, core: 2. Of those that a mesh axis runs over, the one named last changes fastest.
Arguments:
- tokens: bfloat16 [512, 6144], P('row', 'col'), may hold values from -6 to 6
- out_grad: bfloat16 [512, 6144], P('row', 'col'), may hold values from -6 to 6
- pre_act: bfloat16 [512, 24576], P('col', 'row'), may hold values from -6 to 6
- w_in: bfloat16 [6144, 24576], P('col', 'row'), may hold values from -0.078125 to 0.078125
- w_out: bfloat16 [24576, 6144], P('row', 'col'), may hold values from -0.0390625 to 0.0390625
Outputs:
- grad_tokens: bfloat16 [512, 6144], P('row', 'col')
- grad_w_in: bfloat16 [6144, 24576], P('col', 'row')
- grad_w_out: bfloat16 [24576, 6144], P('row', 'col')
All inputs are finite; a program needn't handle non-finite values.
Results may differ from a plain program's by a relative error of at most 0.03.
Values may be sent and summed in bfloat16 or wider, within the bound.
A program may use at most 128 MiB of HBM per device.

v0:
```python
import math

import jax
import jax.numpy as jnp
from jax import lax
from jax.sharding import PartitionSpec as P

gelu_coef = math.sqrt(2.0 / math.pi)
cubic_coef = 0.044715


def gelu_parts(pre_values):
    pre_f32 = pre_values.astype(jnp.float32)
    tangent = jnp.tanh(gelu_coef * (pre_f32 + cubic_coef * pre_f32 * pre_f32 * pre_f32))
    activated = 0.5 * pre_f32 * (1.0 + tangent)
    slopes = 0.5 * (1.0 + tangent) + 0.5 * pre_f32 * (1.0 - tangent * tangent) * gelu_coef * (
        1.0 + 3.0 * cubic_coef * pre_f32 * pre_f32
    )
    return (activated, slopes)


def contract(left_side, right_side, left_dim, right_dim):
    return lax.dot_general(
        left_side,
        right_side,
        (((left_dim,), (right_dim,)), ((), ())),
        preferred_element_type=jnp.float32,
    )


def body(tokens, out_grad, pre_act, w_in, w_out):
    tok_all, grad_all = (
        lax.all_gather(tokens, "row", axis=0, tiled=True),
        lax.all_gather(out_grad, "row", axis=0, tiled=True),
    )
    row_block = grad_all
    hidden_grad = lax.psum_scatter(
        contract(row_block, w_out, 1, 1).astype(jnp.bfloat16),
        "col",
        scatter_dimension=0,
        tiled=True,
    ).astype(jnp.float32)
    activated, slopes = gelu_parts(pre_act)
    hidden_share = activated.astype(jnp.bfloat16)
    pregrad_share = (hidden_grad * slopes).astype(jnp.bfloat16)
    hid_all, pregrad_all = (
        lax.all_gather(hidden_share, "col", axis=0, tiled=True),
        lax.all_gather(pregrad_share, "col", axis=0, tiled=True),
    )
    grad_scale = float(tok_all.shape[0]) ** (-0.5)
    grad_w_out = (contract(hid_all, grad_all, 0, 0) * grad_scale).astype(jnp.bfloat16)
    grad_w_in = (contract(tok_all, pregrad_all, 0, 0) * grad_scale).astype(jnp.bfloat16)
    row_block = pregrad_all
    grad_tokens = lax.psum_scatter(
        contract(row_block, w_in, 1, 1).astype(jnp.bfloat16), "row", scatter_dimension=0, tiled=True
    )
    return (grad_tokens, grad_w_in, grad_w_out)


def solution(mesh):
    in_specs = (P("row", "col"), P("row", "col"), P("col", "row"), P("col", "row"), P("row", "col"))
    out_specs = (P("row", "col"), P("col", "row"), P("row", "col"))
    return jax.shard_map(body, mesh=mesh, in_specs=in_specs, out_specs=out_specs, check_vma=False)
```

profile of v0, /device:TPU:1, one launch (start us, length us, event | category | flops | bytes accessed | tf_op | source)
XLA Modules:
  0.0 378.7 jit_solution(12443934171988346401)
XLA Ops:
  7.2 0.0 reduce-scatter.3.cloned.1.call-start
  7.2 10.2 %all_gather.12 = bf16[512,768]{1,0:T(8,128)(2,1)S(1)} all-gather(bf16[128,768]{1,0:T(8,128)(2,1)} %param.6), channel_id=1, replica_groups=mesh['row'=4,'col'=8] {'row'}, dimensions={0}, use_global_device_ids=true | all-gather | bytes 983040 | tf_op jit(solution)/shard_map/all_gather | solution.py:34
  17.4 10.6 %convolution_convert_fusion = bf16[512,6144]{1,0:T(8,128)(2,1)} fusion(bf16[512,768]{1,0:T(8,128)(2,1)S(1)} %all_gather.12, bf16[6144,768]{1,0:T(8,128)(2,1)} %param.9), kind=kOutput, calls=%fused_computation.3 | convolution fusion | flops 4834983936 | bytes 16515072 | tf_op jit(solution)/shard_map/dot_general | solution.py:23
  28.0 0.0 copy-start
  28.0 0.0 copy-start.1
  28.0 0.0 reduce-scatter.3.cloned.1.call-update
  28.0 0.0 all-gather.3.cloned.1.call-start
  28.1 117.6 %reduce-scatter.3.cloned.1.call-done = bf16[64,6144]{1,0:T(8,128)(2,1)} async-done(((bf16[512,6144]{1,0:T(8,128)(2,1)}), bf16[64,6144]{1,0:T(8,128)(2,1)}) %reduce-scatter.3.cloned.1.call-update) | async-done | bytes 786448 | tf_op jit(solution)/shard_map/reduce_scatter | solution.py:37
  145.7 0.0 copy-done
  145.7 3.4 fusion.8
  149.1 0.0 all-gather.3.cloned.1.call-update
  149.2 0.0 all-gather.5.cloned.1.call-start
  149.2 0.7 all-gather.5.cloned.1.call-update
  149.9 0.0 reduce-scatter.5.cloned.1.call-start
  150.0 0.0 copy-done.1
  150.0 9.9 %all_gather.14 = bf16[512,768]{1,0:T(8,128)(2,1)S(1)} all-gather(bf16[128,768]{1,0:T(8,128)(2,1)S(1)} %copy-done.1), channel_id=1, replica_groups=mesh['row'=4,'col'=8] {'row'}, dimensions={0}, use_global_device_ids=true | all-gather | bytes 983040 | tf_op jit(solution)/shard_map/all_gather | solution.py:33
  159.8 87.9 %all-gather.3.cloned.1.call-done = bf16[512,6144]{1,0:T(8,128)(2,1)} async-done(((bf16[64,6144]{1,0:T(8,128)(2,1)}), bf16[512,6144]{1,0:T(8,128)(2,1)}) %all-gather.3.cloned.1.call-update) | async-done | bytes 6291472 | tf_op jit(solution)/shard_map/all_gather | solution.py:48
  247.8 10.7 %convolution_convert_fusion.1 = bf16[512,768]{1,0:T(8,128)(2,1)} fusion(bf16[512,6144]{1,0:T(8,128)(2,1)} %all-gather.3.cloned.1.call-done, bf16[768,6144]{1,0:T(8,128)(2,1)} %param.8), kind=kOutput, calls=%fused_computation.22 | convolution fusion | flops 4832231424 | bytes 16515072 | tf_op jit(solution)/shard_map/dot_general | solution.py:23
  258.4 0.0 reduce-scatter.5.cloned.1.call-update
  258.5 10.1 %fusion = bf16[768,6144]{0,1:T(8,128)(2,1)} fusion(bf16[512,6144]{1,0:T(8,128)(2,1)} %all-gather.3.cloned.1.call-done, bf16[512,768]{1,0:T(8,128)(2,1)S(1)} %all_gather.14), kind=kOutput, calls=%fused_computation.2 | convolution fusion | flops 4841275392 | bytes 16515072 | tf_op jit(solution)/shard_map/dot_general | solution.py:23
  268.6 12.6 %copy.8 = bf16[768,6144]{1,0:T(8,128)(2,1)} copy(bf16[768,6144]{0,1:T(8,128)(2,1)} %fusion) | data formatting | bytes 18874368
  281.2 66.0 %all-gather.5.cloned.1.call-done = bf16[512,6144]{1,0:T(8,128)(2,1)} async-done(((bf16[64,6144]{1,0:T(8,128)(2,1)}), bf16[512,6144]{1,0:T(8,128)(2,1)}) %all-gather.5.cloned.1.call-update) | async-done | bytes 6291472 | tf_op jit(solution)/shard_map/all_gather | solution.py:47
  347.2 10.1 %multiply_convert_fusion = bf16[6144,768]{1,0:T(8,128)(2,1)} fusion(bf16[512,6144]{1,0:T(8,128)(2,1)} %all-gather.5.cloned.1.call-done, bf16[512,768]{1,0:T(8,128)(2,1)S(1)} %all_gather.12), kind=kOutput, calls=%fused_computation | convolution fusion | flops 4841275392 | bytes 16515072 | tf_op jit(solution)/shard_map/dot_general | solution.py:23
  357.3 14.9 %reduce-scatter.5.cloned.1.call-done = bf16[128,768]{1,0:T(8,128)(2,1)} async-done(((bf16[512,768]{1,0:T(8,128)(2,1)}), bf16[128,768]{1,0:T(8,128)(2,1)}) %reduce-scatter.5.cloned.1.call-update) | async-done | bytes 196624 | tf_op jit(solution)/shard_map/reduce_scatter | solution.py:54
Async XLA Ops:
  7.2 138.5 %reduce-scatter.3.cloned.1.call-start = ((), (), s32[]{:S(2)}) async-start(), calls=%async_computation.2 | async-start | bytes 7077888 | tf_op jit(solution)/shard_map/reduce_scatter | solution.py:37
  28.0 117.7 %copy-start = (bf16[64,6144]{1,0:T(8,128)(2,1)S(1)}, bf16[64,6144]{1,0:T(8,128)(2,1)}, u32[]{:S(2)}) copy-start(bf16[64,6144]{1,0:T(8,128)(2,1)} %param.7) | copy-start | bytes 2359300
  28.0 122.0 %copy-start.1 = (bf16[128,768]{1,0:T(8,128)(2,1)S(1)}, bf16[128,768]{1,0:T(8,128)(2,1)}, u32[]{:S(2)}) copy-start(bf16[128,768]{1,0:T(8,128)(2,1)} %param.5) | copy-start | bytes 589828
  28.0 219.7 %all-gather.3.cloned.1.call-start = ((), (), s32[]{:S(2)}) async-start(), calls=%async_computation.3 | async-start | bytes 7077888 | tf_op jit(solution)/shard_map/all_gather | solution.py:48
  149.2 198.0 %all-gather.5.cloned.1.call-start = ((), (), s32[]{:S(2)}) async-start(), calls=%async_computation.5 | async-start | bytes 7077888 | tf_op jit(solution)/shard_map/all_gather | solution.py:47
  149.9 222.2 %reduce-scatter.5.cloned.1.call-start = ((), (), s32[]{:S(2)}) async-start(), calls=%async_computation.4 | async-start | bytes 983040 | tf_op jit(solution)/shard_map/reduce_scatter | solution.py:54
Sparse Core Ops, SparseCore 0:
  28.1 117.5 reduce-scatter.2
  149.3 98.4 all-gather.2
  250.0 97.1 all-gather.4
  350.2 21.9 reduce-scatter.4
where the time goes:
time: 380 us; the launch traced here: 379 us
  waiting for transfers between devices  287 us (76%)
  matrix products  41.5 us (11%)
  blocking collectives  20 us (5%)
  between operations  13.8 us (4%)
  local copies, waits for them, and re-layouts  12.6 us (3%)
    reduce_scatter x1, waiting for transfers between devices, body(): lax.psum_scatter(contract(row_block, w_out, 1, 1).astype(jnp.bfloat16), '...  118 us
    all_gather x1, waiting for transfers between devices, body(): lax.all_gather(pregrad_share, 'col', axis=0, tiled=True)  87.9 us
    all_gather x1, waiting for transfers between devices, body(): lax.all_gather(hidden_share, 'col', axis=0, tiled=True)  66 us
    dot_general x4, matrix products, contract(): lax.dot_general(left_side, right_side, (((left_dim,), (right_dim,)), ((),...  41.5 us
    reduce_scatter x1, waiting for transfers between devices, body(): lax.psum_scatter(contract(row_block, w_in, 1, 1).astype(jnp.bfloat16), 'r...  14.9 us
    unnamed x5, local copies, waits for them, and re-layouts  12.6 us
    all_gather x1, blocking collectives, body(): lax.all_gather(out_grad, 'row', axis=0, tiled=True)  10.2 us
    all_gather x1, blocking collectives, body(): lax.all_gather(tokens, 'row', axis=0, tiled=True)  9.86 us
  transfers between devices with their start and end apart: 4, of which 4 were waited for; matrix products, arithmetic and copies ran while one was open for 11% of the time, Pallas kernels for 0%

commit v1 on v0

v1 whole, which is shorter than its diff:
```python
import functools
import math

import jax
import jax.numpy as jnp
from jax import lax
from jax.experimental import pallas as pl
from jax.experimental.pallas import tpu as pltpu
from jax.sharding import PartitionSpec as P

gelu_coef = math.sqrt(2.0 / math.pi)
cubic_coef = 0.044715
MESH = pl.DeviceIdType.MESH
CHUNKS = 4


def gelu_parts(pre_f32):
    tangent = jnp.tanh(gelu_coef * (pre_f32 + cubic_coef * pre_f32 * pre_f32 * pre_f32))
    activated = 0.5 * pre_f32 * (1.0 + tangent)
    slopes = 0.5 * (1.0 + tangent) + 0.5 * pre_f32 * (1.0 - tangent * tangent) * gelu_coef * (
        1.0 + 3.0 * cubic_coef * pre_f32 * pre_f32
    )
    return (activated, slopes)


def contract(left_side, right_side, left_dim, right_dim):
    return lax.dot_general(
        left_side,
        right_side,
        (((left_dim,), (right_dim,)), ((), ())),
        preferred_element_type=jnp.float32,
    )


def exchange_kernel(
    n_row, n_col,
    tok_ref, grad_ref, pre_ref, w_ref,
    tok_all, grad_all, act_all, pg_all,
    g_v, w_v, h_v, a_v, p_v, in_v, slope_v,
    w_sem, own_sem, out_sem,
    g_send, g_recv, x_send, x_recv,
    h_send, h_recv, a_send, a_recv, p_send, p_recv,
):
    rows = grad_ref.shape[0]
    share = pre_ref.shape[0]
    width = w_v.shape[1]
    tile = 256 if width % 256 == 0 else 128
    last = n_col - 2
    row = lax.axis_index("row")
    col = lax.axis_index("col")
    odd = col % 2
    pos = (1 - odd) * (col // 2) + odd * (n_col - 1 - col // 2)

    def col_at(place):
        place = (place + 2 * n_col) % n_col
        back = place // (n_col // 2)
        return (1 - back) * (2 * place) + back * (2 * (n_col - 1 - place) + 1)

    def row_slice(index, size):
        return pl.ds(pl.multiple_of(index * size, size), size)

    def sign(q):
        return 1 if q % 2 == 0 else -1

    def ring(q, src, dst, send_sem, recv_sem):
        return pltpu.make_async_remote_copy(
            src_ref=src, dst_ref=dst, send_sem=send_sem, recv_sem=recv_sem,
            device_id=(row, col_at(pos + sign(q))), device_id_type=MESH,
        )

    def h_copy(q, step):
        return ring(q, in_v.at[q, step], in_v.at[q, step + 1], h_send.at[q, step + 1], h_recv.at[q, step + 1])

    def h_arrival(q, step):
        block = in_v.at[q, step]
        return ring(q, block, block, h_send.at[q, step], h_recv.at[q, step])

    def h_first(q):
        block = h_v.at[q, row_slice(col_at(pos - sign(q)), share)]
        return ring(q, block, in_v.at[q, 0], h_send.at[q, 0], h_recv.at[q, 0])

    def gather_copy(buf, send_sem, recv_sem, q, step):
        block = buf.at[q, row_slice(col_at(pos - sign(q) * step), share)]
        return ring(q, block, block, send_sem.at[q, step], recv_sem.at[q, step])

    def gather_arrival(buf, send_sem, recv_sem, q, step):
        block = buf.at[q, row_slice(col_at(pos - sign(q) * (step + 1)), share)]
        return ring(q, block, block, send_sem.at[q, step], recv_sem.at[q, step])

    a_ring = (a_v, a_send, a_recv)
    p_ring = (p_v, p_send, p_recv)

    w_loads = [
        pltpu.make_async_copy(w_ref.at[pl.ds(q * width, width)], w_v.at[q], w_sem.at[q])
        for q in range(CHUNKS)
    ]
    for load in w_loads:
        load.start()

    barrier = pltpu.get_barrier_semaphore()
    for k in range(1, n_row):
        pl.semaphore_signal(barrier, inc=1, device_id=((row + k) % n_row, col), device_id_type=MESH)
    for side in (1, -1):
        pl.semaphore_signal(barrier, inc=1, device_id=(row, col_at(pos + side)), device_id_type=MESH)
    pl.semaphore_wait(barrier, n_row + 1)

    def row_copy(src, dst, send_sem, recv_sem, k, owner):
        return pltpu.make_async_remote_copy(
            src_ref=src, dst_ref=dst.at[row_slice(owner, rows)],
            send_sem=send_sem.at[k - 1], recv_sem=recv_sem.at[k - 1],
            device_id=((row + k) % n_row, col), device_id_type=MESH,
        )

    for k in range(1, n_row):
        row_copy(grad_ref, g_v, g_send, g_recv, k, row).start()
    g_v[row_slice(row, rows), :] = grad_ref[...]

    for q in range(CHUNKS):
        @pl.loop(0, width // tile)
        def _(j, q=q):
            lanes = pl.ds(pl.multiple_of(j * tile, tile), tile)
            source = pl.ds(pl.multiple_of(q * width + j * tile, 128), tile)
            activated, slopes = gelu_parts(pre_ref[:, source].astype(jnp.float32))
            a_v[q, row_slice(col, share), lanes] = activated.astype(jnp.bfloat16)
            slope_v[q, :, lanes] = slopes

        gather_copy(*a_ring, q, 0).start()

    for k in range(1, n_row):
        row_copy(grad_ref, g_v, g_send, g_recv, k, (row + n_row - k) % n_row).wait_recv()

    for q in range(CHUNKS):
        w_loads[q].wait()

        @pl.loop(0, width // tile)
        def _(j, q=q):
            lanes = pl.ds(pl.multiple_of(j * tile, tile), tile)
            h_v[q, :, lanes] = contract(g_v[...], w_v[q, lanes, :], 1, 1).astype(jnp.bfloat16)

        h_first(q).start()

    for k in range(1, n_row):
        row_copy(tok_ref, tok_all, x_send, x_recv, k, row).start()
    own_tokens = pltpu.make_async_copy(tok_ref, tok_all.at[row_slice(row, rows)], own_sem.at[0])
    own_tokens.start()
    grad_out = pltpu.make_async_copy(g_v, grad_all, own_sem.at[1])
    grad_out.start()

    @pl.loop(0, last)
    def _(step):
        for q in range(CHUNKS):
            h_arrival(q, step).wait_recv()
            own = h_v[q, row_slice(col_at(pos - sign(q) * (step + 2)), share), :]
            total = in_v[q, step].astype(jnp.float32) + own.astype(jnp.float32)
            in_v[q, step] = total.astype(jnp.bfloat16)
            h_copy(q, step).start()
            gather_arrival(*a_ring, q, step).wait_recv()
            gather_copy(*a_ring, q, step + 1).start()

    for q in range(CHUNKS):
        h_arrival(q, last).wait_recv()
        mine = row_slice(col, share)
        total = in_v[q, last].astype(jnp.float32) + h_v[q, mine, :].astype(jnp.float32)
        p_v[q, mine, :] = (total * slope_v[q]).astype(jnp.bfloat16)
        gather_copy(*p_ring, q, 0).start()

    def write_out(buf, out, q, which):
        return pltpu.make_async_copy(
            buf.at[q], out.at[:, pl.ds(q * width, width)], out_sem.at[which, q]
        )

    for q in range(CHUNKS):
        gather_arrival(*a_ring, q, last).wait_recv()
        write_out(a_v, act_all, q, 0).start()

    @pl.loop(0, last)
    def _(step):
        for q in range(CHUNKS):
            gather_arrival(*p_ring, q, step).wait_recv()
            gather_copy(*p_ring, q, step + 1).start()

    for q in range(CHUNKS):
        gather_arrival(*p_ring, q, last).wait_recv()
        write_out(p_v, pg_all, q, 1).start()

    for k in range(1, n_row):
        row_copy(grad_ref, g_v, g_send, g_recv, k, row).wait_send()
        row_copy(tok_ref, tok_all, x_send, x_recv, k, row).wait_send()
        row_copy(tok_ref, tok_all, x_send, x_recv, k, (row + n_row - k) % n_row).wait_recv()
    own_tokens.wait()
    grad_out.wait()

    for q in range(CHUNKS):
        h_first(q).wait_send()

        @pl.loop(0, last)
        def _(step, q=q):
            h_copy(q, step).wait_send()

        @pl.loop(0, last + 1)
        def _(step, q=q):
            gather_copy(*a_ring, q, step).wait_send()
            gather_copy(*p_ring, q, step).wait_send()

        write_out(a_v, act_all, q, 0).wait()
        write_out(p_v, pg_all, q, 1).wait()


def body(n_row, n_col, tokens, out_grad, pre_act, w_in, w_out):
    rows, depth = tokens.shape
    share, units = pre_act.shape
    total = rows * n_row
    width = units // CHUNKS
    half = jnp.bfloat16
    dma = pltpu.SemaphoreType.DMA
    ring_sem = dma((CHUNKS, n_col - 1))
    row_sem = dma((n_row - 1,))
    vmem = pl.BlockSpec(memory_space=pltpu.VMEM)
    anywhere = pl.BlockSpec(memory_space=pl.ANY)
    tok_all, grad_all, hid_all, pregrad_all = pl.pallas_call(
        functools.partial(exchange_kernel, n_row, n_col),
        out_shape=(
            jax.ShapeDtypeStruct((total, depth), half),
            jax.ShapeDtypeStruct((total, depth), half),
            jax.ShapeDtypeStruct((total, units), half),
            jax.ShapeDtypeStruct((total, units), half),
        ),
        in_specs=[vmem, vmem, vmem, anywhere],
        out_specs=(anywhere,) * 4,
        scratch_shapes=[
            pltpu.VMEM((total, depth), half),
            pltpu.VMEM((CHUNKS, width, depth), half),
            pltpu.VMEM((CHUNKS, total, width), half),
            pltpu.VMEM((CHUNKS, total, width), half),
            pltpu.VMEM((CHUNKS, total, width), half),
            pltpu.VMEM((CHUNKS, n_col - 1, share, width), half),
            pltpu.VMEM((CHUNKS, share, width), jnp.float32),
            dma((CHUNKS,)), dma((2,)), dma((2, CHUNKS)),
            row_sem, row_sem, row_sem, row_sem,
            ring_sem, ring_sem, ring_sem, ring_sem, ring_sem, ring_sem,
        ],
        compiler_params=pltpu.CompilerParams(
            collective_id=0, has_side_effects=True, vmem_limit_bytes=56 * 2**20
        ),
        cost_estimate=pl.CostEstimate(
            flops=2 * total * depth * units, bytes_accessed=40 * 2**20, transcendentals=share * units
        ),
        name="exchange",
    )(tokens, out_grad, pre_act, w_out)
    grad_scale = float(total) ** (-0.5)
    grad_tokens = lax.psum_scatter(
        contract(pregrad_all, w_in, 1, 1).astype(half), "row", scatter_dimension=0, tiled=True
    )
    grad_w_out = (contract(hid_all, grad_all, 0, 0) * grad_scale).astype(half)
    grad_w_in = (contract(tok_all, pregrad_all, 0, 0) * grad_scale).astype(half)
    return (grad_tokens, grad_w_in, grad_w_out)


def solution(mesh):
    in_specs = (P("row", "col"), P("row", "col"), P("col", "row"), P("col", "row"), P("row", "col"))
    out_specs = (P("row", "col"), P("col", "row"), P("row", "col"))
    sizes = (mesh.shape["row"], mesh.shape["col"])
    return jax.shard_map(
        functools.partial(body, *sizes), mesh=mesh, in_specs=in_specs, out_specs=out_specs, check_vma=False
    )
```

time: 380 us -> 239 us (0.63)
  waiting for transfers between devices: 287 us -> 1.83 us
  Pallas kernels: 0 us -> 191 us
  blocking collectives: 20 us -> 0 us
  local copies, waits for them, and re-layouts: 12.6 us -> 0.01 us
  matrix products: 41.5 us -> 31.3 us
    pallas_call x0 -> x1, Pallas kernels: none -> 191 us  [body(): pl.pallas_call(functools.partial(exchange_kernel, n_row, n_col), out_shap...]
    all_gather x2 -> x0, waiting for transfers between devices: 154 us -> none  [the longest x1 87.9 us: body(): lax.all_gather(pregrad_share, 'col', axis=0, tiled=True)]
    reduce_scatter x2 -> x1, waiting for transfers between devices: 133 us -> 1.81 us  [body(): lax.psum_scatter(contract(pregrad_all, w_in, 1, 1).astype(half), 'row', s...]
    all_gather x2 -> x0, blocking collectives: 20 us -> none  [the longest x1 10.2 us: body(): lax.all_gather(out_grad, 'row', axis=0, tiled=True)]
    unnamed x5 -> x4, local copies, waits for them, and re-layouts: 12.6 us -> 0.01 us
    dot_general x4 -> x3, matrix products: 41.5 us -> 31.3 us  [contract(): lax.dot_general(left_side, right_side, (((left_dim,), (right_dim,)), ((),...]
  transfers between devices with their start and end apart: 4 -> 1, of which waited for: 4 -> 1; matrix products, arithmetic and copies ran while one was open for 11% -> 9% of each run, Pallas kernels for 0% -> 0%
where the time goes in v1:
time: 239 us; the launch traced here: 238 us
  Pallas kernels  191 us (80%)
  matrix products  31.3 us (13%)
  between operations  14.1 us (6%)
    pallas_call x1, Pallas kernels, body(): pl.pallas_call(functools.partial(exchange_kernel, n_row, n_col), out_shap...  191 us
    dot_general x3, matrix products, contract(): lax.dot_general(left_side, right_side, (((left_dim,), (right_dim,)), ((),...  31.3 us
  transfers between devices with their start and end apart: 1, of which 1 were waited for; matrix products, arithmetic and copies ran while one was open for 9% of the time, Pallas kernels for 0%

profile of v1, /device:TPU:1, one launch (start us, length us, event | category | flops | bytes accessed | tf_op | source)
XLA Modules:
  0.0 238.3 jit_solution(5711042241494261476)
XLA Ops:
  7.2 0.0 reduce-scatter.2.cloned.1.call-start
  7.2 191.1 %exchange.1 = (bf16[512,768]{1,0:T(8,128)(2,1)}, bf16[512,768]{1,0:T(8,128)(2,1)}, bf16[512,6144]{1,0:T(8,128)(2,1)}, bf16[512,6144]{1,0:T(8,128)(2,1)}) custom-call(bf16[128,768]{1,0:T(8,128)(2,1)} %tok_ref.1, bf16[128,768]{1,0:T(8,128)(2,1)} %grad_ref.1, bf16[64,6144]{1,0:T(8,128)(2,1)} %pre_ref.1, bf16[6144,768]{1,0:T(8,128)(2,1)} %w_ref.1), custom_call_target="tpu_custom_call" | custom-call | flops 4831838208 | bytes 41943040 | tf_op jit(solution)/shard_map/exchange/pallas_call | solution.py:220
  198.3 0.0 copy-start
  198.3 10.8 %convolution_convert_fusion = bf16[512,768]{1,0:T(8,128)(2,1)} fusion(bf16[512,6144]{1,0:T(8,128)(2,1)} %get-tuple-element.7, bf16[768,6144]{1,0:T(8,128)(2,1)} %param.8), kind=kOutput, calls=%fused_computation.2 | convolution fusion | flops 4832231424 | bytes 16515072 | tf_op jit(solution)/shard_map/dot_general | solution.py:27
  209.1 0.0 copy-start.1
  209.1 0.0 reduce-scatter.2.cloned.1.call-update
  209.1 0.0 copy-done
  209.1 10.5 %multiply_convert_fusion.1 = bf16[768,6144]{1,0:T(8,128)(2,1)} fusion(bf16[512,768]{1,0:T(8,128)(2,1)S(1)} %copy-done, bf16[512,6144]{1,0:T(8,128)(2,1)} %get-tuple-element.7), kind=kOutput, calls=%fused_computation.1 | convolution fusion | flops 4841275392 | bytes 16515072 | tf_op jit(solution)/shard_map/dot_general | solution.py:27
  219.6 0.0 copy-done.1
  219.6 10.1 %multiply_convert_fusion = bf16[6144,768]{1,0:T(8,128)(2,1)} fusion(bf16[512,6144]{1,0:T(8,128)(2,1)} %get-tuple-element.9, bf16[512,768]{1,0:T(8,128)(2,1)S(1)} %copy-done.1), kind=kOutput, calls=%fused_computation | convolution fusion | flops 4841275392 | bytes 16515072 | tf_op jit(solution)/shard_map/dot_general | solution.py:27
  229.7 1.8 reduce-scatter.2.cloned.1.call-done
Async XLA Ops:
  7.2 224.3 %reduce-scatter.2.cloned.1.call-start = ((), (), s32[]{:S(2)}) async-start(), calls=%async_computation.1 | async-start | bytes 983040 | tf_op jit(solution)/shard_map/reduce_scatter | solution.py:251
  198.3 10.8 %copy-start = (bf16[512,768]{1,0:T(8,128)(2,1)S(1)}, bf16[512,768]{1,0:T(8,128)(2,1)}, u32[]{:S(2)}) copy-start(bf16[512,768]{1,0:T(8,128)(2,1)} %get-tuple-element.8) | copy-start | bytes 2359300
  209.1 10.6 %copy-start.1 = (bf16[512,768]{1,0:T(8,128)(2,1)S(1)}, bf16[512,768]{1,0:T(8,128)(2,1)}, u32[]{:S(2)}) copy-start(bf16[512,768]{1,0:T(8,128)(2,1)} %get-tuple-element.10) | copy-start | bytes 2359300
Sparse Core Ops, SparseCore 0:
  209.2 22.2 reduce-scatter.1

commit v2 on v1

--- a/solution.py
+++ b/solution.py
@@ -34,10 +34,10 @@
 
 def exchange_kernel(
     n_row, n_col,
-    tok_ref, grad_ref, pre_ref, w_ref,
-    tok_all, grad_all, act_all, pg_all,
-    g_v, w_v, h_v, a_v, p_v, in_v, slope_v,
-    w_sem, own_sem, out_sem,
+    tok_ref, grad_ref, pre_ref, w_ref, w_in_ref,
+    tok_all, grad_all, act_all, pg_all, gt_ref,
+    g_v, w_v, h_v, a_v, p_v, in_v, slope_v, wi_v, part_v, terms_v,
+    w_sem, wi_sem, own_sem, out_sem, t_send, t_recv,
     g_send, g_recv, x_send, x_recv,
     h_send, h_recv, a_send, a_recv, p_send, p_recv,
 ):
@@ -111,9 +111,38 @@
             device_id=((row + k) % n_row, col), device_id_type=MESH,
         )
 
-    for k in range(1, n_row):
-        row_copy(grad_ref, g_v, g_send, g_recv, k, row).start()
+    pairs = n_row // 2
+    sibling = row + 1 - 2 * (row % 2)
+
+    def peer(m):
+        return (row + 2 * m) % n_row
+
+    def source_of(m):
+        return (row + n_row - 2 * m) % n_row
+
+    def grad_copy(index, src, owner, target):
+        return pltpu.make_async_remote_copy(
+            src_ref=src, dst_ref=g_v.at[row_slice(owner, rows)],
+            send_sem=g_send.at[index], recv_sem=g_recv.at[index],
+            device_id=(target, col), device_id_type=MESH,
+        )
+
+    def grad_arrival(index, owner):
+        return grad_copy(index, grad_ref, owner, sibling)
+
+    def grad_relay(m):
+        owner = source_of(m)
+        return grad_copy(pairs - 1 + m, g_v.at[row_slice(owner, rows)], owner, sibling)
+
+    for m in range(1, pairs):
+        grad_copy(m, grad_ref, row, peer(m)).start()
+    grad_copy(0, grad_ref, row, sibling).start()
     g_v[row_slice(row, rows), :] = grad_ref[...]
+
+    def forward_activated(step):
+        for q in range(CHUNKS):
+            gather_arrival(*a_ring, q, step).wait_recv()
+            gather_copy(*a_ring, q, step + 1).start()
 
     for q in range(CHUNKS):
         @pl.loop(0, width // tile)
@@ -125,9 +154,14 @@
             slope_v[q, :, lanes] = slopes
 
         gather_copy(*a_ring, q, 0).start()
-
-    for k in range(1, n_row):
-        row_copy(grad_ref, g_v, g_send, g_recv, k, (row + n_row - k) % n_row).wait_recv()
+        if q == 1:
+            for m in range(1, pairs):
+                grad_arrival(m, source_of(m)).wait_recv()
+                grad_relay(m).start()
+
+    grad_arrival(0, sibling).wait_recv()
+    for m in range(1, pairs):
+        grad_arrival(pairs - 1 + m, (sibling + n_row - 2 * m) % n_row).wait_recv()
 
     for q in range(CHUNKS):
         w_loads[q].wait()
@@ -138,6 +172,15 @@
             h_v[q, :, lanes] = contract(g_v[...], w_v[q, lanes, :], 1, 1).astype(jnp.bfloat16)
 
         h_first(q).start()
+        if q % 2 == 1:
+            forward_activated(q // 2)
+
+    wi_loads = [
+        pltpu.make_async_copy(w_in_ref.at[:, pl.ds(q * width, width)], wi_v.at[q], wi_sem.at[q])
+        for q in range(CHUNKS)
+    ]
+    for load in wi_loads:
+        load.start()
 
     for k in range(1, n_row):
         row_copy(tok_ref, tok_all, x_send, x_recv, k, row).start()
@@ -146,16 +189,26 @@
     grad_out = pltpu.make_async_copy(g_v, grad_all, own_sem.at[1])
     grad_out.start()
 
-    @pl.loop(0, last)
+    def add_and_pass(q, step):
+        h_arrival(q, step).wait_recv()
+        own = h_v[q, row_slice(col_at(pos - sign(q) * (step + 2)), share), :]
+        total = in_v[q, step].astype(jnp.float32) + own.astype(jnp.float32)
+        in_v[q, step] = total.astype(jnp.bfloat16)
+        h_copy(q, step).start()
+
+    ahead = CHUNKS // 2
+
+    @pl.loop(0, last - ahead)
     def _(step):
         for q in range(CHUNKS):
-            h_arrival(q, step).wait_recv()
-            own = h_v[q, row_slice(col_at(pos - sign(q) * (step + 2)), share), :]
-            total = in_v[q, step].astype(jnp.float32) + own.astype(jnp.float32)
-            in_v[q, step] = total.astype(jnp.bfloat16)
-            h_copy(q, step).start()
-            gather_arrival(*a_ring, q, step).wait_recv()
-            gather_copy(*a_ring, q, step + 1).start()
+            add_and_pass(q, step)
+            gather_arrival(*a_ring, q, step + ahead).wait_recv()
+            gather_copy(*a_ring, q, step + ahead + 1).start()
+
+    @pl.loop(last - ahead, last)
+    def _(step):
+        for q in range(CHUNKS):
+            add_and_pass(q, step)
 
     for q in range(CHUNKS):
         h_arrival(q, last).wait_recv()
@@ -182,9 +235,41 @@
     for q in range(CHUNKS):
         gather_arrival(*p_ring, q, last).wait_recv()
         write_out(p_v, pg_all, q, 1).start()
-
+        wi_loads[q].wait()
+
+    def term_copy(j, k):
+        target = (row + k) % n_row
+        return pltpu.make_async_remote_copy(
+            src_ref=part_v.at[j, row_slice(target, rows)], dst_ref=terms_v.at[j, k - 1],
+            send_sem=t_send.at[j, k - 1], recv_sem=t_recv.at[j, k - 1],
+            device_id=(target, col), device_id_type=MESH,
+        )
+
+    slabs, slab = part_v.shape[0], part_v.shape[2]
+    for j in range(slabs):
+        lines = pl.ds(j * slab, slab)
+        total = contract(p_v[0], wi_v[0, lines, :], 1, 1)
+        for q in range(1, CHUNKS):
+            total = total + contract(p_v[q], wi_v[q, lines, :], 1, 1)
+        part_v[j] = total.astype(jnp.bfloat16)
+        for k in range(1, n_row):
+            term_copy(j, k).start()
+
+    for j in range(slabs):
+        total = part_v[j, row_slice(row, rows), :].astype(jnp.float32)
+        for k in range(1, n_row):
+            term_copy(j, k).wait_recv()
+            total = total + terms_v[j, k - 1].astype(jnp.float32)
+        gt_ref[:, pl.ds(j * slab, slab)] = total.astype(jnp.bfloat16)
+
+    for j in range(slabs):
+        for k in range(1, n_row):
+            term_copy(j, k).wait_send()
+    grad_copy(0, grad_ref, row, sibling).wait_send()
+    for m in range(1, pairs):
+        grad_copy(m, grad_ref, row, peer(m)).wait_send()
+        grad_relay(m).wait_send()
     for k in range(1, n_row):
-        row_copy(grad_ref, g_v, g_send, g_recv, k, row).wait_send()
         row_copy(tok_ref, tok_all, x_send, x_recv, k, row).wait_send()
         row_copy(tok_ref, tok_all, x_send, x_recv, k, (row + n_row - k) % n_row).wait_recv()
     own_tokens.wait()
@@ -211,22 +296,24 @@
     share, units = pre_act.shape
     total = rows * n_row
     width = units // CHUNKS
+    slab = 256 if depth % 256 == 0 else 128
     half = jnp.bfloat16
     dma = pltpu.SemaphoreType.DMA
     ring_sem = dma((CHUNKS, n_col - 1))
     row_sem = dma((n_row - 1,))
     vmem = pl.BlockSpec(memory_space=pltpu.VMEM)
     anywhere = pl.BlockSpec(memory_space=pl.ANY)
-    tok_all, grad_all, hid_all, pregrad_all = pl.pallas_call(
+    tok_all, grad_all, hid_all, pregrad_all, grad_tokens = pl.pallas_call(
         functools.partial(exchange_kernel, n_row, n_col),
         out_shape=(
             jax.ShapeDtypeStruct((total, depth), half),
             jax.ShapeDtypeStruct((total, depth), half),
             jax.ShapeDtypeStruct((total, units), half),
             jax.ShapeDtypeStruct((total, units), half),
+            jax.ShapeDtypeStruct((rows, depth), half),
         ),
-        in_specs=[vmem, vmem, vmem, anywhere],
-        out_specs=(anywhere,) * 4,
+        in_specs=[vmem, vmem, vmem, anywhere, anywhere],
+        out_specs=(anywhere,) * 4 + (vmem,),
         scratch_shapes=[
             pltpu.VMEM((total, depth), half),
             pltpu.VMEM((CHUNKS, width, depth), half),
@@ -235,22 +322,23 @@
             pltpu.VMEM((CHUNKS, total, width), half),
             pltpu.VMEM((CHUNKS, n_col - 1, share, width), half),
             pltpu.VMEM((CHUNKS, share, width), jnp.float32),
-            dma((CHUNKS,)), dma((2,)), dma((2, CHUNKS)),
+            pltpu.VMEM((CHUNKS, depth, width), half),
+            pltpu.VMEM((depth // slab, total, slab), half),
+            pltpu.VMEM((depth // slab, n_row - 1, rows, slab), half),
+            dma((CHUNKS,)), dma((CHUNKS,)), dma((2,)), dma((2, CHUNKS)),
+            dma((depth // slab, n_row - 1)), dma((depth // slab, n_row - 1)),
             row_sem, row_sem, row_sem, row_sem,
             ring_sem, ring_sem, ring_sem, ring_sem, ring_sem, ring_sem,
         ],
         compiler_params=pltpu.CompilerParams(
-            collective_id=0, has_side_effects=True, vmem_limit_bytes=56 * 2**20
+            collective_id=0, has_side_effects=True, vmem_limit_bytes=58 * 2**20
         ),
         cost_estimate=pl.CostEstimate(
             flops=2 * total * depth * units, bytes_accessed=40 * 2**20, transcendentals=share * units
         ),
         name="exchange",
-    )(tokens, out_grad, pre_act, w_out)
+    )(tokens, out_grad, pre_act, w_out, w_in)
     grad_scale = float(total) ** (-0.5)
-    grad_tokens = lax.psum_scatter(
-        contract(pregrad_all, w_in, 1, 1).astype(half), "row", scatter_dimension=0, tiled=True
-    )
     grad_w_out = (contract(hid_all, grad_all, 0, 0) * grad_scale).astype(half)
     grad_w_in = (contract(tok_all, pregrad_all, 0, 0) * grad_scale).astype(half)
     return (grad_tokens, grad_w_in, grad_w_out)

time: 239 us -> 222 us (0.929)
  matrix products: 31.3 us -> 17.4 us
  between operations: 14.1 us -> 0.68 us
  Pallas kernels: 191 us -> 203 us
    dot_general x3 -> x2, matrix products: 31.3 us -> 17.4 us  [contract(): lax.dot_general(left_side, right_side, (((left_dim,), (right_dim,)), ((),...]
    pallas_call x1, Pallas kernels: 191 us -> 203 us  [body(): pl.pallas_call(functools.partial(exchange_kernel, n_row, n_col), out_shap...]
  transfers between devices with their start and end apart: 1 -> 0, of which waited for: 1 -> 0; matrix products, arithmetic and copies ran while one was open for 9% -> 0% of each run, Pallas kernels for 0% -> 0%
where the time goes in v2:
time: 222 us
  Pallas kernels  203 us (91%)
  matrix products  17.4 us (8%)
    pallas_call x1, Pallas kernels, body(): pl.pallas_call(functools.partial(exchange_kernel, n_row, n_col), out_shap...  203 us
    dot_general x2, matrix products, contract(): lax.dot_general(left_side, right_side, (((left_dim,), (right_dim,)), ((),...  17.4 us

profile of v2, /device:TPU:1, one launch (start us, length us, event | category | flops | bytes accessed | tf_op | source)
XLA Modules:
  0.0 222.2 jit_solution(391050500069076638)
XLA Ops:
  0.6 203.4 %exchange.1 = (bf16[512,768]{1,0:T(8,128)(2,1)}, bf16[512,768]{1,0:T(8,128)(2,1)}, bf16[512,6144]{1,0:T(8,128)(2,1)}, bf16[512,6144]{1,0:T(8,128)(2,1)}, bf16[128,768]{1,0:T(8,128)(2,1)}) custom-call(bf16[128,768]{1,0:T(8,128)(2,1)} %tok_ref.1, bf16[128,768]{1,0:T(8,128)(2,1)} %grad_ref.1, bf16[64,6144]{1,0:T(8,128)(2,1)} %pre_ref.1, ...), custom_call_target="tpu_custom_call" | custom-call | flops 4831838208 | bytes 41943040 | tf_op jit(solution)/shard_map/exchange/pallas_call | solution.py:306
  204.0 0.0 slice-start
  204.0 0.0 copy-start.1
  204.0 0.0 slice-start.1
  204.1 9.8 %multiply_convert_fusion.1 = bf16[768,6144]{1,0:T(8,128)(2,1)} fusion(bf16[512,768]{1,0:T(8,128)(2,1)} %get-tuple-element.9, bf16[512,6144]{1,0:T(8,128)(2,1)} %get-tuple-element.10), kind=kOutput, calls=%fused_computation.1 | convolution fusion | flops 4841275392 | bytes 16515072 | tf_op jit(solution)/shard_map/dot_general | solution.py:27
  213.8 0.0 slice-done
  213.8 0.0 copy-done.1
  213.8 0.0 slice-done.1
  213.8 0.0 copy-start
  213.9 7.6 %multiply_convert_fusion = bf16[6144,768]{1,0:T(8,128)(2,1)} fusion(bf16[512,6144]{1,0:T(8,128)(2,1)S(1)} %bitcast.5, bf16[512,768]{1,0:T(8,128)(2,1)S(1)} %copy-done.1), kind=kOutput, calls=%fused_computation | convolution fusion | flops 4841275392 | bytes 16515072 | tf_op jit(solution)/shard_map/dot_general | solution.py:27
  221.5 0.0 copy-done
  221.5 0.7 copy.9
  (1 shorter events, 0.0 us)
Async XLA Ops:
  204.0 9.8 %slice-start = ((s8[6291456]{0:T(1024)(128)(4,1)}), s8[4194304]{0:T(1024)(128)(4,1)S(1)}, s32[]{:S(2)}) async-start(s8[6291456]{0:T(1024)(128)(4,1)} %bitcast.4), calls=%async_computation | async-start | bytes 8388608
  204.0 9.8 %copy-start.1 = (bf16[512,768]{1,0:T(8,128)(2,1)S(1)}, bf16[512,768]{1,0:T(8,128)(2,1)}, u32[]{:S(2)}) copy-start(bf16[512,768]{1,0:T(8,128)(2,1)} %get-tuple-element.12) | copy-start | bytes 2359300
  204.0 9.8 %slice-start.1 = ((s8[6291456]{0:T(1024)(128)(4,1)}), s8[2097152]{0:T(1024)(128)(4,1)S(1)}, s32[]{:S(2)}) async-start(s8[6291456]{0:T(1024)(128)(4,1)} %bitcast.4), calls=%async_computation.1 | async-start | bytes 4194304
  213.8 7.6 %copy-start = (bf16[128,768]{1,0:T(8,128)(2,1)S(1)}, bf16[128,768]{1,0:T(8,128)(2,1)}, u32[]{:S(2)}) copy-start(bf16[128,768]{1,0:T(8,128)(2,1)} %get-tuple-element.16) | copy-start | bytes 589828

commit v3 on v2

--- a/solution.py
+++ b/solution.py
@@ -289,6 +289,45 @@
 
         write_out(a_v, act_all, q, 0).wait()
         write_out(p_v, pg_all, q, 1).wait()
+
+
+def weight_kernel(scale, tok_ref, grad_ref, act_ref, pg_ref, w_in_ref, w_out_ref, tok_t):
+    @pl.when(pl.program_id(0) == 0)
+    def _():
+        tok_t[...] = tok_ref[...].T
+
+    w_out_ref[...] = (contract(act_ref[...], grad_ref[...], 0, 0) * scale).astype(jnp.bfloat16)
+    w_in_ref[...] = (contract(tok_t[...], pg_ref[...], 1, 0) * scale).astype(jnp.bfloat16)
+
+
+def weight_grads(tok_all, grad_all, hid_all, pregrad_all):
+    total, depth = tok_all.shape
+    units = hid_all.shape[1]
+    tile = 512 if units % 512 == 0 else 128
+    scale = float(total) ** (-0.5)
+    whole = pl.BlockSpec((total, depth), lambda i: (0, 0))
+    columns = pl.BlockSpec((total, tile), lambda i: (0, i))
+    return pl.pallas_call(
+        functools.partial(weight_kernel, scale),
+        grid=(units // tile,),
+        out_shape=(
+            jax.ShapeDtypeStruct((depth, units), jnp.bfloat16),
+            jax.ShapeDtypeStruct((units, depth), jnp.bfloat16),
+        ),
+        in_specs=[whole, whole, columns, columns],
+        out_specs=(
+            pl.BlockSpec((depth, tile), lambda i: (0, i)),
+            pl.BlockSpec((tile, depth), lambda i: (i, 0)),
+        ),
+        scratch_shapes=[pltpu.VMEM((depth, total), jnp.bfloat16)],
+        compiler_params=pltpu.CompilerParams(vmem_limit_bytes=56 * 2**20),
+        cost_estimate=pl.CostEstimate(
+            flops=4 * total * depth * units,
+            bytes_accessed=4 * units * (total + depth) + 4 * total * depth,
+            transcendentals=0,
+        ),
+        name="weight_grads",
+    )(tok_all, grad_all, hid_all, pregrad_all)
 
 
 def body(n_row, n_col, tokens, out_grad, pre_act, w_in, w_out):
@@ -338,9 +377,7 @@
         ),
         name="exchange",
     )(tokens, out_grad, pre_act, w_out, w_in)
-    grad_scale = float(total) ** (-0.5)
-    grad_w_out = (contract(hid_all, grad_all, 0, 0) * grad_scale).astype(half)
-    grad_w_in = (contract(tok_all, pregrad_all, 0, 0) * grad_scale).astype(half)
+    grad_w_in, grad_w_out = weight_grads(tok_all, grad_all, hid_all, pregrad_all)
     return (grad_tokens, grad_w_in, grad_w_out)
 
 

time: 222 us -> 223 us (level)
  Pallas kernels: 203 us -> 221 us
  matrix products: 17.4 us -> 0 us
    pallas_call x0 -> x1, Pallas kernels: none -> 18 us  [weight_grads(): pl.pallas_call(functools.partial(weight_kernel, scale), grid=(units // ti...]
    dot_general x2 -> x0, matrix products: 17.4 us -> none  [contract(): lax.dot_general(left_side, right_side, (((left_dim,), (right_dim,)), ((),...]
where the time goes in v3:
time: 223 us
  Pallas kernels  221 us (99%)
    pallas_call x1, Pallas kernels, body(): pl.pallas_call(functools.partial(exchange_kernel, n_row, n_col), out_shap...  203 us
    pallas_call x1, Pallas kernels, weight_grads(): pl.pallas_call(functools.partial(weight_kernel, scale), grid=(units // ti...  18 us

profile of v3, /device:TPU:1, one launch (start us, length us, event | category | flops | bytes accessed | tf_op | source)
XLA Modules:
  0.0 222.8 jit_solution(17068896658368556917)
XLA Ops:
  0.6 203.4 %exchange.1 = (bf16[512,768]{1,0:T(8,128)(2,1)}, bf16[512,768]{1,0:T(8,128)(2,1)}, bf16[512,6144]{1,0:T(8,128)(2,1)}, bf16[512,6144]{1,0:T(8,128)(2,1)}, bf16[128,768]{1,0:T(8,128)(2,1)}) custom-call(bf16[128,768]{1,0:T(8,128)(2,1)} %tok_ref.1, bf16[128,768]{1,0:T(8,128)(2,1)} %grad_ref.1, bf16[64,6144]{1,0:T(8,128)(2,1)} %pre_ref.1, ...), custom_call_target="tpu_custom_call" | custom-call | flops 4831838208 | bytes 41943040 | tf_op jit(solution)/shard_map/exchange/pallas_call | solution.py:345
  204.0 0.0 copy-start
  204.0 18.0 %weight_grads.1 = (bf16[768,6144]{1,0:T(8,128)(2,1)}, bf16[6144,768]{1,0:T(8,128)(2,1)}) custom-call(bf16[512,768]{1,0:T(8,128)(2,1)} %get-tuple-element.11.tok_ref, bf16[512,768]{1,0:T(8,128)(2,1)} %get-tuple-element.12.grad_ref, bf16[512,6144]{1,0:T(8,128)(2,1)} %get-tuple-element.13.act_ref, bf16[512,6144]{1,0:T(8,128)(2,1)} %get-tuple-element.14.pg_ref), custom_call_target="tpu_custom_call" | custom-call | flops 9663676416 | bytes 33030144 | tf_op jit(solution)/shard_map/weight_grads/pallas_call | solution.py:310
  222.1 0.0 copy-done
  222.1 0.7 copy.9
Async XLA Ops:
  204.0 18.1 %copy-start = (bf16[128,768]{1,0:T(8,128)(2,1)S(1)}, bf16[128,768]{1,0:T(8,128)(2,1)}, u32[]{:S(2)}) copy-start(bf16[128,768]{1,0:T(8,128)(2,1)} %get-tuple-element.20) | copy-start | bytes 589828

commit v4 on v2

--- a/solution.py
+++ b/solution.py
@@ -172,8 +172,8 @@
             h_v[q, :, lanes] = contract(g_v[...], w_v[q, lanes, :], 1, 1).astype(jnp.bfloat16)
 
         h_first(q).start()
-        if q % 2 == 1:
-            forward_activated(q // 2)
+        if q == 1:
+            forward_activated(0)
 
     wi_loads = [
         pltpu.make_async_copy(w_in_ref.at[:, pl.ds(q * width, width)], wi_v.at[q], wi_sem.at[q])
@@ -196,19 +196,13 @@
         in_v[q, step] = total.astype(jnp.bfloat16)
         h_copy(q, step).start()
 
-    ahead = CHUNKS // 2
-
-    @pl.loop(0, last - ahead)
-    def _(step):
+    @pl.loop(0, last // 2)
+    def _(turn):
         for q in range(CHUNKS):
-            add_and_pass(q, step)
-            gather_arrival(*a_ring, q, step + ahead).wait_recv()
-            gather_copy(*a_ring, q, step + ahead + 1).start()
-
-    @pl.loop(last - ahead, last)
-    def _(step):
+            add_and_pass(q, 2 * turn)
+        forward_activated(turn + 1)
         for q in range(CHUNKS):
-            add_and_pass(q, step)
+            add_and_pass(q, 2 * turn + 1)
 
     for q in range(CHUNKS):
         h_arrival(q, last).wait_recv()
@@ -222,15 +216,22 @@
             buf.at[q], out.at[:, pl.ds(q * width, width)], out_sem.at[which, q]
         )
 
-    for q in range(CHUNKS):
-        gather_arrival(*a_ring, q, last).wait_recv()
-        write_out(a_v, act_all, q, 0).start()
-
-    @pl.loop(0, last)
-    def _(step):
+    def forward_pre_grad(step):
         for q in range(CHUNKS):
             gather_arrival(*p_ring, q, step).wait_recv()
             gather_copy(*p_ring, q, step + 1).start()
+
+    @pl.loop(0, last // 2 - 1)
+    def _(turn):
+        forward_pre_grad(2 * turn)
+        forward_activated(last // 2 + 1 + turn)
+        forward_pre_grad(2 * turn + 1)
+
+    forward_pre_grad(last - 2)
+    for q in range(CHUNKS):
+        gather_arrival(*a_ring, q, last).wait_recv()
+        write_out(a_v, act_all, q, 0).start()
+    forward_pre_grad(last - 1)
 
     for q in range(CHUNKS):
         gather_arrival(*p_ring, q, last).wait_recv()

time: 222 us -> 222 us (level)
  no operation moved by 1% of the time
where the time goes in v4:
time: 222 us
  Pallas kernels  203 us (91%)
  matrix products  17.4 us (8%)
    pallas_call x1, Pallas kernels, body(): pl.pallas_call(functools.partial(exchange_kernel, n_row, n_col), out_shap...  203 us
    dot_general x2, matrix products, contract(): lax.dot_general(left_side, right_side, (((left_dim,), (right_dim,)), ((),...  17.4 us

profile of v4, /device:TPU:1, one launch (start us, length us, event | category | flops | bytes accessed | tf_op | source)
XLA Modules:
  0.0 222.2 jit_solution(13312534626811175403)
XLA Ops:
  0.6 203.4 %exchange.1 = (bf16[512,768]{1,0:T(8,128)(2,1)}, bf16[512,768]{1,0:T(8,128)(2,1)}, bf16[512,6144]{1,0:T(8,128)(2,1)}, bf16[512,6144]{1,0:T(8,128)(2,1)}, bf16[128,768]{1,0:T(8,128)(2,1)}) custom-call(bf16[128,768]{1,0:T(8,128)(2,1)} %tok_ref.1, bf16[128,768]{1,0:T(8,128)(2,1)} %grad_ref.1, bf16[64,6144]{1,0:T(8,128)(2,1)} %pre_ref.1, ...), custom_call_target="tpu_custom_call" | custom-call | flops 4831838208 | bytes 41943040 | tf_op jit(solution)/shard_map/exchange/pallas_call | solution.py:307
  204.0 0.0 slice-start
  204.0 0.0 copy-start.1
  204.0 0.0 slice-start.1
  204.1 9.8 %multiply_convert_fusion.1 = bf16[768,6144]{1,0:T(8,128)(2,1)} fusion(bf16[512,768]{1,0:T(8,128)(2,1)} %get-tuple-element.9, bf16[512,6144]{1,0:T(8,128)(2,1)} %get-tuple-element.10), kind=kOutput, calls=%fused_computation.1 | convolution fusion | flops 4841275392 | bytes 16515072 | tf_op jit(solution)/shard_map/dot_general | solution.py:27
  213.8 0.0 slice-done
  213.8 0.0 copy-done.1
  213.8 0.0 slice-done.1
  213.8 0.0 copy-start
  213.9 7.6 %multiply_convert_fusion = bf16[6144,768]{1,0:T(8,128)(2,1)} fusion(bf16[512,6144]{1,0:T(8,128)(2,1)S(1)} %bitcast.5, bf16[512,768]{1,0:T(8,128)(2,1)S(1)} %copy-done.1), kind=kOutput, calls=%fused_computation | convolution fusion | flops 4841275392 | bytes 16515072 | tf_op jit(solution)/shard_map/dot_general | solution.py:27
  221.5 0.0 copy-done
  221.5 0.7 copy.9
  (1 shorter events, 0.0 us)
Async XLA Ops:
  204.0 9.8 %slice-start = ((s8[6291456]{0:T(1024)(128)(4,1)}), s8[4194304]{0:T(1024)(128)(4,1)S(1)}, s32[]{:S(2)}) async-start(s8[6291456]{0:T(1024)(128)(4,1)} %bitcast.4), calls=%async_computation | async-start | bytes 8388608
  204.0 9.8 %copy-start.1 = (bf16[512,768]{1,0:T(8,128)(2,1)S(1)}, bf16[512,768]{1,0:T(8,128)(2,1)}, u32[]{:S(2)}) copy-start(bf16[512,768]{1,0:T(8,128)(2,1)} %get-tuple-element.12) | copy-start | bytes 2359300
  204.0 9.8 %slice-start.1 = ((s8[6291456]{0:T(1024)(128)(4,1)}), s8[2097152]{0:T(1024)(128)(4,1)S(1)}, s32[]{:S(2)}) async-start(s8[6291456]{0:T(1024)(128)(4,1)} %bitcast.4), calls=%async_computation.1 | async-start | bytes 4194304
  213.8 7.6 %copy-start = (bf16[128,768]{1,0:T(8,128)(2,1)S(1)}, bf16[128,768]{1,0:T(8,128)(2,1)}, u32[]{:S(2)}) copy-start(bf16[128,768]{1,0:T(8,128)(2,1)} %get-tuple-element.16) | copy-start | bytes 589828

commit v5 on v4

--- a/solution.py
+++ b/solution.py
@@ -36,7 +36,7 @@
     n_row, n_col,
     tok_ref, grad_ref, pre_ref, w_ref, w_in_ref,
     tok_all, grad_all, act_all, pg_all, gt_ref,
-    g_v, w_v, h_v, a_v, p_v, in_v, slope_v, wi_v, part_v, terms_v,
+    g_v, w_v, h_v, a_v, p_v, in_v, slope_v, wi_v, part_v, terms_v, acc_v,
     w_sem, wi_sem, own_sem, out_sem, t_send, t_recv,
     g_send, g_recv, x_send, x_recv,
     h_send, h_recv, a_send, a_recv, p_send, p_recv,
@@ -237,6 +237,10 @@
         gather_arrival(*p_ring, q, last).wait_recv()
         write_out(p_v, pg_all, q, 1).start()
         wi_loads[q].wait()
+        if q < CHUNKS - 1:
+            for j in range(part_v.shape[0]):
+                piece = contract(p_v[q], wi_v[q, pl.ds(j * part_v.shape[2], part_v.shape[2]), :], 1, 1)
+                acc_v[j] = piece if q == 0 else acc_v[j] + piece
 
     def term_copy(j, k):
         target = (row + k) % n_row
@@ -249,9 +253,7 @@
     slabs, slab = part_v.shape[0], part_v.shape[2]
     for j in range(slabs):
         lines = pl.ds(j * slab, slab)
-        total = contract(p_v[0], wi_v[0, lines, :], 1, 1)
-        for q in range(1, CHUNKS):
-            total = total + contract(p_v[q], wi_v[q, lines, :], 1, 1)
+        total = acc_v[j] + contract(p_v[CHUNKS - 1], wi_v[CHUNKS - 1, lines, :], 1, 1)
         part_v[j] = total.astype(jnp.bfloat16)
         for k in range(1, n_row):
             term_copy(j, k).start()
@@ -326,6 +328,7 @@
             pltpu.VMEM((CHUNKS, depth, width), half),
             pltpu.VMEM((depth // slab, total, slab), half),
             pltpu.VMEM((depth // slab, n_row - 1, rows, slab), half),
+            pltpu.VMEM((depth // slab, total, slab), jnp.float32),
             dma((CHUNKS,)), dma((CHUNKS,)), dma((2,)), dma((2, CHUNKS)),
             dma((depth // slab, n_row - 1)), dma((depth // slab, n_row - 1)),
             row_sem, row_sem, row_sem, row_sem,

time: 222 us -> 220 us (level)
  no operation moved by 1% of the time
where the time goes in v5:
time: 220 us
  Pallas kernels  201 us (91%)
  matrix products  17.6 us (8%)
    pallas_call x1, Pallas kernels, body(): pl.pallas_call(functools.partial(exchange_kernel, n_row, n_col), out_shap...  201 us
    dot_general x2, matrix products, contract(): lax.dot_general(left_side, right_side, (((left_dim,), (right_dim,)), ((),...  17.6 us

profile of v5, /device:TPU:1, one launch (start us, length us, event | category | flops | bytes accessed | tf_op | source)
XLA Modules:
  0.0 220.3 jit_solution(148712067554537864)
XLA Ops:
  0.6 201.3 %exchange.1 = (bf16[512,768]{1,0:T(8,128)(2,1)}, bf16[512,768]{1,0:T(8,128)(2,1)}, bf16[512,6144]{1,0:T(8,128)(2,1)}, bf16[512,6144]{1,0:T(8,128)(2,1)}, bf16[128,768]{1,0:T(8,128)(2,1)}) custom-call(bf16[128,768]{1,0:T(8,128)(2,1)} %tok_ref.1, bf16[128,768]{1,0:T(8,128)(2,1)} %grad_ref.1, bf16[64,6144]{1,0:T(8,128)(2,1)} %pre_ref.1, ...), custom_call_target="tpu_custom_call" | custom-call | flops 4831838208 | bytes 41943040 | tf_op jit(solution)/shard_map/exchange/pallas_call | solution.py:309
  202.0 0.0 slice-start
  202.0 0.0 copy-start.1
  202.0 0.0 slice-start.1
  202.0 9.8 %multiply_convert_fusion.1 = bf16[768,6144]{1,0:T(8,128)(2,1)} fusion(bf16[512,768]{1,0:T(8,128)(2,1)} %get-tuple-element.9, bf16[512,6144]{1,0:T(8,128)(2,1)} %get-tuple-element.10), kind=kOutput, calls=%fused_computation.1 | convolution fusion | flops 4841275392 | bytes 16515072 | tf_op jit(solution)/shard_map/dot_general | solution.py:27
  211.8 0.0 slice-done
  211.8 0.0 copy-done.1
  211.8 0.0 slice-done.1
  211.8 0.0 copy-start
  211.8 7.8 %multiply_convert_fusion = bf16[6144,768]{1,0:T(8,128)(2,1)} fusion(bf16[512,6144]{1,0:T(8,128)(2,1)S(1)} %bitcast.5, bf16[512,768]{1,0:T(8,128)(2,1)S(1)} %copy-done.1), kind=kOutput, calls=%fused_computation | convolution fusion | flops 4841275392 | bytes 16515072 | tf_op jit(solution)/shard_map/dot_general | solution.py:27
  219.6 0.0 copy-done
  219.6 0.7 copy.9
  (1 shorter events, 0.0 us)
Async XLA Ops:
  202.0 9.8 %slice-start = ((s8[6291456]{0:T(1024)(128)(4,1)}), s8[4194304]{0:T(1024)(128)(4,1)S(1)}, s32[]{:S(2)}) async-start(s8[6291456]{0:T(1024)(128)(4,1)} %bitcast.4), calls=%async_computation | async-start | bytes 8388608
  202.0 9.8 %copy-start.1 = (bf16[512,768]{1,0:T(8,128)(2,1)S(1)}, bf16[512,768]{1,0:T(8,128)(2,1)}, u32[]{:S(2)}) copy-start(bf16[512,768]{1,0:T(8,128)(2,1)} %get-tuple-element.12) | copy-start | bytes 2359300
  202.0 9.8 %slice-start.1 = ((s8[6291456]{0:T(1024)(128)(4,1)}), s8[2097152]{0:T(1024)(128)(4,1)S(1)}, s32[]{:S(2)}) async-start(s8[6291456]{0:T(1024)(128)(4,1)} %bitcast.4), calls=%async_computation.1 | async-start | bytes 4194304
  211.8 7.8 %copy-start = (bf16[128,768]{1,0:T(8,128)(2,1)S(1)}, bf16[128,768]{1,0:T(8,128)(2,1)}, u32[]{:S(2)}) copy-start(bf16[128,768]{1,0:T(8,128)(2,1)} %get-tuple-element.16) | copy-start | bytes 589828
